TPU v7x, 768 devices: a whole 4x8x12 slice. The times are simulated.
768 devices in a mesh: dp: 12 (over z_lo, x), seq: 32 (over y, z_hi), grp: 2 (over core).
Axes of the slice: x: 4, y: 8, z: 12 (z_hi: 4, z_lo: 3; z = z_hi * 3 + z_lo), core: 2. Of those that a mesh axis runs over, the one named last changes fastest.
Arguments:
- text_proj: bfloat16 [3, 384, 12, 128, 128], P(None, 'dp', None, ('seq', 'grp')), may hold values from -50 to 50
- image_proj: bfloat16 [3, 384, 12, 160, 128], P(None, ('dp', 'seq'), None, 'grp'), may hold values from -50 to 50
- text_grad: bfloat16 [384, 12, 128, 128], P('dp', None, ('seq', 'grp')), may hold values from -15 to 15
- image_grad: bfloat16 [384, 12, 160, 128], P(('dp', 'seq'), None, 'grp'), may hold values from -15 to 15
- text_lengths: int32 [384], P(('dp', 'seq')), may hold values from 1 to 128
- norm_gains: float32 [2, 2, 128], replicated, may hold values from 0.7 to 5.2
Outputs:
- text_out: bfloat16 [384, 12, 128, 128], P('dp', None, ('seq', 'grp'))
- image_out: bfloat16 [384, 12, 160, 128], P(('dp', 'seq'), None, 'grp')
- text_proj_grad: bfloat16 [3, 384, 12, 128, 128], P(None, 'dp', None, ('seq', 'grp'))
- image_proj_grad: bfloat16 [3, 384, 12, 160, 128], P(None, ('dp', 'seq'), None, 'grp')
- gain_grad: float32 [2, 2, 128], replicated
All inputs are finite; a program needn't handle non-finite values.
Results may differ from a plain program's by a relative error of at most 0.025.
The roundings to bfloat16 on the way count: a program that leaves them out, or rounds other values in their place, can miss the bound.
Values may be sent and summed in bfloat16 or wider, within the bound.
A program may use at most 32 MiB of HBM per device.

v0:
```python
import functools

import jax
import jax.numpy as jnp
from jax import lax
from jax.sharding import Mesh
from jax.sharding import PartitionSpec as P

TXT = 128
SEQ = ("seq_0", "seq_1")
DP_SEQ_GRP = ("dp_0", "dp_1", "seq_0", "seq_1", "grp")
DP = ("dp_0", "dp_1")
SEQ_GRP = ("seq_0", "seq_1", "grp")
DP_SEQ = ("dp_0", "dp_1", "seq_0", "seq_1")


EPSILON = 1e-06
MASKED = -1e30


def in_one_piece(arrays, axis, split_dim, concat_dim, along):
    both = jnp.concatenate(arrays, axis=along)
    out, at, gathered = (
        lax.all_to_all(both, axis, split_axis=split_dim, concat_axis=concat_dim, tiled=True),
        0,
        [],
    )
    for a in arrays:
        gathered.append(lax.slice_in_dim(out, at, at + a.shape[along], axis=along))
        at += a.shape[along]
    return tuple(gathered)


def in_blocks(shard, dim, count):
    lengths = shard.shape
    blocks = shard.reshape(*lengths[:dim], count, lengths[dim] // count, *lengths[dim + 1 :])
    return jnp.moveaxis(blocks, dim, 0)


def edges_of(length, count):
    unit = 8 if length >= 8 * count else 1
    return [length // unit * k // count * unit for k in range(1, count)]


def in_order(blocks, dim):
    lengths = list(blocks.shape[1:])
    lengths[dim] *= blocks.shape[0]
    return jnp.moveaxis(blocks, 0, dim).reshape(lengths)


def cut_exchange(shard, axis, pieces, split_dim, concat_dim):
    blocks = in_blocks(shard, split_dim, lax.axis_size(axis))
    split_at = max(range(1, max(2, blocks.ndim - 1)), key=lambda d: blocks.shape[d])
    gathered = []
    for share in jnp.split(blocks, edges_of(blocks.shape[split_at], pieces), axis=split_at):
        if share.size:
            gathered.append(lax.all_to_all(share, axis, split_axis=0, concat_axis=0, tiled=True))
    return in_order(jnp.concatenate(gathered, axis=split_at), concat_dim)


def one_axis_at_a_time(shard, axes):
    return functools.reduce(lax.psum, axes, shard)


def forward(queries, key_rows, value_rows, key_valid):
    factor = queries.shape[-1] ** (-0.5)
    scores = (
        jnp.einsum("nqd,nkd->nqk", queries, key_rows, preferred_element_type=jnp.float32) * factor
    )
    scores = jnp.where(key_valid[:, None, :], scores, MASKED)
    row_max = jnp.max(scores, axis=-1, keepdims=True)
    exponent = jnp.exp(scores - row_max)
    attn_probs = exponent / jnp.sum(exponent, axis=-1, keepdims=True)
    rounded_probs = attn_probs.astype(jnp.bfloat16)
    attn_local = jnp.einsum(
        "nqk,nkd->nqd", rounded_probs, value_rows, preferred_element_type=jnp.float32
    )
    return (attn_probs, rounded_probs, attn_local)


def backward_terms(queries, key_rows, value_rows, attn_probs, rounded_probs, grad_out):
    factor = queries.shape[-1] ** (-0.5)
    grad_value = jnp.einsum(
        "nqk,nqd->nkd", rounded_probs, grad_out, preferred_element_type=jnp.float32
    )
    grad_probs = jnp.einsum(
        "nqd,nkd->nqk", grad_out, value_rows, preferred_element_type=jnp.float32
    )
    row_delta = jnp.sum(attn_probs * grad_probs, axis=-1, keepdims=True)
    grad_scores = (attn_probs * (grad_probs - row_delta) * factor).astype(jnp.bfloat16)
    grad_query = jnp.einsum(
        "nqk,nkd->nqd", grad_scores, key_rows, preferred_element_type=jnp.float32
    ).astype(jnp.bfloat16)
    grad_key = jnp.einsum("nqk,nqd->nkd", grad_scores, queries, preferred_element_type=jnp.float32)
    return (grad_query, grad_key, grad_value)


def sums_item(packed):
    query_one, key_one, value_one, valid_one, grad_one = packed
    attn_probs, rounded_probs, attn_local = forward(
        query_one[None], key_one[None], value_one[None], valid_one[None]
    )
    grad_query, grad_key, grad_value = backward_terms(
        query_one[None], key_one[None], value_one[None], attn_probs, rounded_probs, grad_one[None]
    )
    return (attn_local[0].astype(jnp.bfloat16), grad_query[0], grad_key[0], grad_value[0])


def whole_item(packed):
    attn_local, grad_query, grad_key, grad_value = sums_item(packed)
    return (attn_local, grad_query, grad_key.astype(jnp.bfloat16), grad_value.astype(jnp.bfloat16))


def unit_parts(raw_bf):
    raw_vals = raw_bf.astype(jnp.float32)
    inverse = lax.rsqrt(jnp.mean(raw_vals * raw_vals, axis=-1, keepdims=True) + EPSILON)
    return (raw_vals * inverse, inverse)


def raw_gradient(grad_normed_bf, unit_vec, inverse, gain_rows):
    grad_normed = grad_normed_bf.astype(jnp.float32)
    gain_part = jnp.sum(grad_normed * unit_vec, axis=(1, 2, 3))
    grad_unit = grad_normed * gain_rows
    grad_raw = inverse * (
        grad_unit - unit_vec * jnp.mean(grad_unit * unit_vec, axis=-1, keepdims=True)
    )
    return (grad_raw.astype(jnp.bfloat16), gain_part)


def global_position(local_row, owner_index, text_rows, text_group, image_rows, grp_count):
    text_place = (
        local_row // text_group * grp_count + owner_index
    ) * text_group + local_row % text_group
    image_place = TXT + owner_index * image_rows + (local_row - text_rows)
    return jnp.where(local_row < text_rows, text_place, image_place)


def per_device(text_proj, image_proj, text_grad, image_grad, text_lengths, norm_gains):
    seq_count = lax.axis_size(SEQ)
    grp_count = lax.axis_size("grp")
    sample_count, head_count, image_rows, head_size = image_grad.shape
    text_group = text_proj.shape[3]
    text_rows = text_group * seq_count
    local_len = text_rows + image_rows
    text_unit, text_inverse = unit_parts(text_proj[:2])
    image_unit, image_inverse = unit_parts(image_proj[:2])
    text_gain = norm_gains[0][:, None, None, None, :]
    image_gain = norm_gains[1][:, None, None, None, :]
    text_stack = jnp.concatenate(
        [(text_unit * text_gain).astype(jnp.bfloat16), text_proj[2:]], axis=0
    )
    image_stack = jnp.concatenate(
        [(image_unit * image_gain).astype(jnp.bfloat16), image_proj[2:]], axis=0
    )
    text_here, text_cot = in_one_piece((text_stack, text_grad[None]), SEQ, 1, 3, 0)
    joint_rows = jnp.concatenate([text_here, image_stack], axis=3)
    cotangent_rows = jnp.concatenate([text_cot[0], image_grad], axis=2)
    key_row = jnp.arange(local_len * grp_count, dtype=jnp.int32)
    key_place = global_position(
        key_row % local_len, key_row // local_len, text_rows, text_group, image_rows, grp_count
    )
    key_valid = (key_place[None, :] >= TXT) | (key_place[None, :] < text_lengths[:, None])
    full_len = local_len * grp_count
    moved_rows, moved_cot = in_one_piece((joint_rows, cotangent_rows[None]), "grp", 2, 3, 0)
    head_share = moved_rows.shape[2]
    item_count = sample_count * head_share
    flat_rows = moved_rows.reshape(3, item_count, full_len, head_size)
    item_valid = jnp.broadcast_to(
        key_valid[:, None, :], (sample_count, head_share, full_len)
    ).reshape(item_count, full_len)
    attn_local, grad_query, grad_key, grad_value = lax.map(
        whole_item,
        (
            flat_rows[0],
            flat_rows[1],
            flat_rows[2],
            item_valid,
            moved_cot.reshape(item_count, full_len, head_size),
        ),
    )
    results = jnp.stack([attn_local, grad_query, grad_key, grad_value]).reshape(
        4, sample_count, head_share, full_len, head_size
    )
    placed = lax.all_to_all(results, "grp", split_axis=3, concat_axis=2, tiled=True)
    text_back = cut_exchange(placed[:, :, :, :text_rows], SEQ, 2, 3, 1)
    image_back = placed[:, :, :, text_rows:]
    text_raw, text_part = raw_gradient(text_back[1:3], text_unit, text_inverse, text_gain)
    image_raw, image_part = raw_gradient(image_back[1:3], image_unit, image_inverse, image_gain)
    partial_value = jnp.stack([text_part, image_part])
    summed_gain = one_axis_at_a_time(partial_value, DP_SEQ_GRP)
    gain_grad = summed_gain / (sample_count * lax.axis_size(DP) * seq_count)
    text_proj_grad = jnp.concatenate([text_raw, text_back[3:]], axis=0)
    image_proj_grad = jnp.concatenate([image_raw, image_back[3:]], axis=0)
    return (text_back[0], image_back[0], text_proj_grad, image_proj_grad, gain_grad)


def solution(mesh):
    torus = Mesh(
        mesh.devices.reshape(3, 4, 8, 4, mesh.shape["grp"]),
        ("dp_0", "dp_1", "seq_0", "seq_1", "grp"),
    )
    in_specs = (
        P(None, DP, None, SEQ_GRP, None),
        P(None, DP_SEQ, None, "grp", None),
        P(DP, None, SEQ_GRP, None),
        P(DP_SEQ, None, "grp", None),
        P(DP_SEQ),
        P(),
    )
    out_specs = (
        P(DP, None, SEQ_GRP, None),
        P(DP_SEQ, None, "grp", None),
        P(None, DP, None, SEQ_GRP, None),
        P(None, DP_SEQ, None, "grp", None),
        P(),
    )
    return jax.shard_map(
        per_device, mesh=torus, in_specs=in_specs, out_specs=out_specs, check_vma=False
    )
```

profile of v0, /device:TPU:1, one launch (start us, length us, event | category | flops | bytes accessed | tf_op | source)
XLA Modules:
  0.0 206.5 jit_solution(17224706206375184866)
XLA Ops:
  0.7 1.3 slice.79
  3.5 1.5 copy.116
  5.0 20.7 %all-to-all-start = ((bf16[4,32,12,2,128]{4,3,2,0,1:T(2,128)(2,1)}), bf16[4,32,12,2,128]{4,3,2,0,1:T(2,128)(2,1)S(1)}, u32[]{:S(2)}, u32[]{:S(2)}) async-start(bf16[4,32,12,2,128]{4,3,2,0,1:T(2,128)(2,1)} %copy.116), calls=%async_computation | async-start | bytes 1572864 | tf_op jit(solution)/shard_map/all_to_all | solution.py:24
  27.3 17.9 %all-to-all-done = bf16[4,32,12,2,128]{4,3,2,0,1:T(2,128)(2,1)S(1)} async-done(((bf16[4,32,12,2,128]{4,3,2,0,1:T(2,128)(2,1)}), bf16[4,32,12,2,128]{4,3,2,0,1:T(2,128)(2,1)S(1)}, u32[]{:S(2)}, u32[]{:S(2)}) %all-to-all-start) | async-done | bytes 786464 | tf_op jit(solution)/shard_map/all_to_all | solution.py:24
  46.7 8.9 %all_to_all.58 = bf16[4,1,12,144,128]{4,3,1,0,2:T(8,128)(2,1)S(1)} all-to-all(bf16[4,1,12,144,128]{4,3,1,0,2:T(8,128)(2,1)S(1)} %pad_maximum_fusion), channel_id=1, replica_groups=mesh['dp_0'=3,'dp_1'=4,'seq_0'=8,'seq_1'=4,'grp'=2] {'grp'}, dimensions={2} | all-to-all | bytes 3538944 | tf_op jit(solution)/shard_map/all_to_all | solution.py:24
  55.9 22.3 %while.16 = (s32[]{:T(128)}, bf16[6,288,128]{2,1,0:T(8,128)(2,1)S(1)}, bf16[6,288,128]{2,1,0:T(8,128)(2,1)}, bf16[6,288,128]{2,1,0:T(8,128)(2,1)}, bf16[6,288,12...) while((s32[]{:T(128)}, ...), condition=%wide.region_6.7_spmd, body=%wide.region_2.6_spmd.sunk | while | flops 129290400 | bytes 4506673 | solution.py:171
  57.5 0.9 fusion.108
  58.4 0.9 fusion.110
  61.2 0.9 fusion.108
  62.1 0.9 fusion.110
  65.0 0.9 fusion.108
  65.9 0.9 fusion.110
  68.7 0.9 fusion.108
  72.4 0.9 fusion.108
  75.3 0.9 fusion.109
  76.1 0.9 fusion.108
  77.0 0.9 fusion.110
  78.2 1.5 maximum_bitcast_fusion
  79.7 1.4 copy.126
  81.1 5.2 %all_to_all.59 = bf16[4,1,6,288,128]{4,0,2,1,3:T(4,128)(2,1)S(1)} all-to-all(bf16[4,1,6,288,128]{4,0,2,1,3:T(4,128)(2,1)S(1)} %copy.126), channel_id=1, replica_groups=mesh['dp_0'=3,'dp_1'=4,'seq_0'=8,'seq_1'=4,'grp'=2] {'grp'}, dimensions={3} | all-to-all | bytes 3538944 | tf_op jit(solution)/shard_map/all_to_all | solution.py:184
  87.2 1.3 fusion.75
  88.5 31.9 %all_to_all.60 = bf16[32,4,1,6,2,128]{5,4,3,2,1,0:T(2,128)(2,1)} all-to-all(bf16[32,4,1,6,2,128]{5,4,3,2,1,0:T(2,128)(2,1)S(1)} %get-tuple-element.125), channel_id=1, replica_groups=mesh['dp_0'=3,'dp_1'=4,'seq_0'=8,'seq_1'=4,'grp'=2] {'seq_0','seq_1'}, dimensions={0} | all-to-all | bytes 786432 | tf_op jit(solution)/shard_map/all_to_all | solution.py:57
  120.4 8.9 %all-to-all-start.4 = ((bf16[32,4,1,6,2,128]{5,4,3,2,1,0:T(2,128)(2,1)}), bf16[32,4,1,6,2,128]{5,4,3,2,1,0:T(2,128)(2,1)S(1)}, u32[]{:S(2)}, u32[]{:S(2)}) async-start(bf16[32,4,1,6,2,128]{5,4,3,2,1,0:T(2,128)(2,1)} %get-tuple-element.126), calls=%async_computation.4 | async-start | bytes 786432 | tf_op jit(solution)/shard_map/all_to_all | solution.py:57
  129.3 0.9 fusion.47
  131.7 0.9 copy.133
  132.7 10.7 %all-to-all-done.4 = bf16[32,4,1,6,2,128]{5,4,3,2,1,0:T(2,128)(2,1)S(1)} async-done(((bf16[32,4,1,6,2,128]{5,4,3,2,1,0:T(2,128)(2,1)}), bf16[32,4,1,6,2,128]{5,4,3,2,1,0:T(2,128)(2,1)S(1)}, u32[]{:S(2)}, u32[]{:S(2)}) %all-to-all-start.4) | async-done | bytes 393248 | tf_op jit(solution)/shard_map/all_to_all | solution.py:57
  144.3 15.8 %psum.35 = f32[2,2,128]{2,1,0:T(2,128)S(1)} all-reduce(f32[2,2,128]{2,1,0:T(2,128)S(1)} %pad_maximum_fusion.4), channel_id=1, replica_groups=mesh['dp_0'=3,'dp_1'=4,'seq_0'=8,'seq_1'=4,'grp'=2] {'dp_0'}, use_global_device_ids=true, to_apply=%region_11.12 | all-reduce | flops 512 | bytes 4096 | tf_op jit(solution)/shard_map/psum | solution.py:62
  160.1 8.4 %psum.36 = f32[2,2,128]{2,1,0:T(2,128)S(1)} all-reduce(f32[2,2,128]{2,1,0:T(2,128)S(1)} %psum.35), channel_id=1, replica_groups=mesh['dp_0'=3,'dp_1'=4,'seq_0'=8,'seq_1'=4,'grp'=2] {'dp_1'}, use_global_device_ids=true, to_apply=%region_12.13 | all-reduce | flops 512 | bytes 4096 | tf_op jit(solution)/shard_map/psum | solution.py:62
  168.5 12.2 %psum.37 = f32[2,2,128]{2,1,0:T(2,128)S(1)} all-reduce(f32[2,2,128]{2,1,0:T(2,128)S(1)} %psum.36), channel_id=1, replica_groups=mesh['dp_0'=3,'dp_1'=4,'seq_0'=8,'seq_1'=4,'grp'=2] {'seq_0'}, use_global_device_ids=true, to_apply=%region_13.14 | all-reduce | flops 512 | bytes 4096 | tf_op jit(solution)/shard_map/psum | solution.py:62
  180.7 10.7 %psum.38 = f32[2,2,128]{2,1,0:T(2,128)S(1)} all-reduce(f32[2,2,128]{2,1,0:T(2,128)S(1)} %psum.37), channel_id=1, replica_groups=mesh['dp_0'=3,'dp_1'=4,'seq_0'=8,'seq_1'=4,'grp'=2] {'seq_1'}, use_global_device_ids=true, to_apply=%region_14.15 | all-reduce | flops 512 | bytes 4096 | tf_op jit(solution)/shard_map/psum | solution.py:62
  191.4 11.8 %psum.39 = f32[2,2,128]{2,1,0:T(2,128)S(1)} all-reduce(f32[2,2,128]{2,1,0:T(2,128)S(1)} %psum.38), channel_id=1, replica_groups=mesh['dp_0'=3,'dp_1'=4,'seq_0'=8,'seq_1'=4,'grp'=2] {'grp'}, use_global_device_ids=true, to_apply=%region_15.16 | all-reduce | flops 512 | bytes 4096 | tf_op jit(solution)/shard_map/psum | solution.py:62
  204.4 1.3 copy.132
  (99 shorter events, 21.7 us)
Async XLA Ops:
  0.6 2.4 %slice-start = ((bf16[3,32,12,2,128]{4,3,2,1,0:T(2,128)(2,1)}), bf16[1,32,12,2,128]{4,3,2,1,0:T(2,128)(2,1)S(1)}, s32[]{:S(2)}) async-start(bf16[3,32,12,2,128]{4,3,2,1,0:T(2,128)(2,1)} %param.8), calls=%async_computation.5 | async-start | bytes 393216 | tf_op jit(solution)/shard_map/slice | solution.py:150
  0.6 2.4 %copy-start.3 = (bf16[32,12,2,128]{3,2,1,0:T(2,128)(2,1)S(1)}, bf16[32,12,2,128]{3,2,1,0:T(2,128)(2,1)}, u32[]{:S(2)}) copy-start(bf16[32,12,2,128]{3,2,1,0:T(2,128)(2,1)} %param.10) | copy-start | bytes 589828
  3.5 22.9 %copy-start = (bf16[3,1,12,80,128]{4,3,2,1,0:T(8,128)(2,1)S(1)}, bf16[3,1,12,80,128]{4,3,2,1,0:T(8,128)(2,1)}, u32[]{:S(2)}) copy-start(bf16[3,1,12,80,128]{4,3,2,1,0:T(8,128)(2,1)} %param.9) | copy-start | bytes 2211844
  5.0 40.2 %all-to-all-start = ((bf16[4,32,12,2,128]{4,3,2,0,1:T(2,128)(2,1)}), bf16[4,32,12,2,128]{4,3,2,0,1:T(2,128)(2,1)S(1)}, u32[]{:S(2)}, u32[]{:S(2)}) async-start(bf16[4,32,12,2,128]{4,3,2,0,1:T(2,128)(2,1)} %copy.116), calls=%async_computation | async-start | bytes 1572864 | tf_op jit(solution)/shard_map/all_to_all | solution.py:24
  27.3 19.2 %copy-start.2 = (bf16[1,12,80,128]{3,2,1,0:T(8,128)(2,1)S(1)}, bf16[1,12,80,128]{3,2,1,0:T(8,128)(2,1)}, u32[]{:S(2)}) copy-start(bf16[1,12,80,128]{3,2,1,0:T(8,128)(2,1)} %param.11) | copy-start | bytes 737284
  120.4 23.0 %all-to-all-start.4 = ((bf16[32,4,1,6,2,128]{5,4,3,2,1,0:T(2,128)(2,1)}), bf16[32,4,1,6,2,128]{5,4,3,2,1,0:T(2,128)(2,1)S(1)}, u32[]{:S(2)}, u32[]{:S(2)}) async-start(bf16[32,4,1,6,2,128]{5,4,3,2,1,0:T(2,128)(2,1)} %get-tuple-element.126), calls=%async_computation.4 | async-start | bytes 786432 | tf_op jit(solution)/shard_map/all_to_all | solution.py:57
  131.6 1.0 copy-start.1
where the time goes:
time: 207 us; the launch traced here: 206 us
  blocking collectives  105 us (51%)
  starting transfers between devices  29.6 us (14%)
  waiting for transfers between devices  28.6 us (14%)
  matrix products  20.6 us (10%)
  local copies, waits for them, and re-layouts  12.9 us (6%)
  other arithmetic  8.04 us (4%)
    psum x5, blocking collectives, one_axis_at_a_time(): return functools.reduce(lax.psum, axes, shard)  59 us
    all_to_all x1, blocking collectives, cut_exchange(): lax.all_to_all(share, axis, split_axis=0, concat_axis=0, tiled=True)  31.9 us
    all_to_all x1, starting transfers between devices, in_one_piece(): lax.all_to_all(both, axis, split_axis=split_dim, concat_axis=concat_dim,...  20.7 us
    all_to_all x1, waiting for transfers between devices, in_one_piece(): lax.all_to_all(both, axis, split_axis=split_dim, concat_axis=concat_dim,...  17.9 us
    all_to_all x1, waiting for transfers between devices, cut_exchange(): lax.all_to_all(share, axis, split_axis=0, concat_axis=0, tiled=True)  10.7 us
    all_to_all x1, starting transfers between devices, cut_exchange(): lax.all_to_all(share, axis, split_axis=0, concat_axis=0, tiled=True)  8.92 us
    all_to_all x1, blocking collectives, in_one_piece(): lax.all_to_all(both, axis, split_axis=split_dim, concat_axis=concat_dim,...  8.85 us
    dot_general x6, matrix products, backward_terms(): jnp.einsum('nqk,nkd->nqd', grad_scores, key_rows, preferred_element_type=...  5.47 us
  transfers between devices with their start and end apart: 2, of which 2 were waited for; matrix products, arithmetic and copies ran while one was open for 2% of the time, Pallas kernels for 0%

commit v1 on v0

v1 whole, which is shorter than its diff:
```python
import functools

import jax
import jax.numpy as jnp
from jax import lax
from jax.experimental import pallas as pl
from jax.experimental.pallas import tpu as pltpu
from jax.sharding import PartitionSpec as P

EPSILON = 1e-06
MASKED = -1e30
MESH_ID = pl.DeviceIdType.MESH
NZ = 4
HEADS_PER_STEP = 2


def dot(a, b, contract_a, contract_b):
    return lax.dot_general(
        a, b, (((contract_a,), (contract_b,)), ((), ())), preferred_element_type=jnp.float32
    )


def unit_parts(raw):
    raw_vals = raw.astype(jnp.float32)
    inverse = lax.rsqrt(jnp.mean(raw_vals * raw_vals, axis=-1, keepdims=True) + EPSILON)
    return raw_vals * inverse, inverse


def attend_head(query_raw, key_raw, value, cotangent, bias, gains, text_rows):
    total, size = query_raw.shape
    factor = size**-0.5

    def gain_rows(c):
        return jnp.concatenate(
            [
                jnp.broadcast_to(gains[0, c][None, :], (text_rows, size)),
                jnp.broadcast_to(gains[1, c][None, :], (total - text_rows, size)),
            ],
            axis=0,
        )

    query_unit, query_inverse = unit_parts(query_raw)
    key_unit, key_inverse = unit_parts(key_raw)
    query_gain, key_gain = gain_rows(0), gain_rows(1)
    query = (query_unit * query_gain).astype(jnp.bfloat16)
    key = (key_unit * key_gain).astype(jnp.bfloat16)

    scores = jnp.where(bias < 0, MASKED, dot(query, key, 1, 1) * factor)
    exponent = jnp.exp(scores - jnp.max(scores, axis=-1, keepdims=True))
    probs = exponent * (1.0 / jnp.sum(exponent, axis=-1, keepdims=True))
    rounded = probs.astype(jnp.bfloat16)
    attention = dot(rounded, value, 1, 0).astype(jnp.bfloat16)
    grad_value = dot(rounded, cotangent, 0, 0).astype(jnp.bfloat16)
    grad_probs = dot(cotangent, value, 1, 1)
    row_delta = jnp.sum(probs * grad_probs, axis=-1, keepdims=True)
    grad_scores = (probs * (grad_probs - row_delta) * factor).astype(jnp.bfloat16)

    def raw_gradient(grad_normed, unit, inverse, gain):
        grad_normed = grad_normed.astype(jnp.bfloat16).astype(jnp.float32)
        term = grad_normed * unit
        text_part = jnp.sum(term[:text_rows], axis=0, keepdims=True)
        image_part = jnp.sum(term[text_rows:], axis=0, keepdims=True)
        mean = jnp.mean(term * gain, axis=-1, keepdims=True)
        grad_raw = inverse * (grad_normed * gain - unit * mean)
        return grad_raw.astype(jnp.bfloat16), text_part, image_part

    grad_query, query_text, query_image = raw_gradient(
        dot(grad_scores, key, 1, 0), query_unit, query_inverse, query_gain
    )
    grad_key, key_text, key_image = raw_gradient(
        dot(grad_scores, query, 0, 0), key_unit, key_inverse, key_gain
    )
    parts = jnp.concatenate([query_text, key_text, query_image, key_image], axis=0)
    return (attention, grad_query, grad_key, grad_value), parts


def kernel(
    sizes,
    text_proj,
    text_grad,
    image_proj,
    image_grad,
    length,
    gains,
    text_out,
    text_proj_grad,
    image_out,
    image_proj_grad,
    gain_out,
    text_in,
    image_in,
    text_res,
    image_res,
    gain_part,
    gain_first,
    gain_mid,
    gain_second,
    text_send,
    text_recv,
    image_send,
    image_recv,
    back_send,
    back_recv,
    image_back_send,
    image_back_recv,
    gain_send,
    gain_recv,
):
    dp_count, seq_count, samples = sizes
    rows_y = seq_count // NZ
    dp, seq, grp = lax.axis_index("dp"), lax.axis_index("seq"), lax.axis_index("grp")
    other = 1 - grp
    owner_count = seq_count * 2
    me = seq * 2 + grp
    heads = text_in.shape[1]
    text_rows = owner_count * text_in.shape[3]
    image_rows = image_proj.shape[3]
    hps = HEADS_PER_STEP
    steps = heads // hps

    def seq_peer(k):
        y = lax.rem(seq // NZ + k // NZ, rows_y)
        z = lax.rem(lax.rem(seq, NZ) + lax.rem(k, NZ), NZ)
        return y * NZ + z

    def peer(k):
        return seq_peer(lax.rem(k, seq_count)), lax.rem(grp + k // seq_count, 2)

    def first_peer(k):
        return lax.rem(dp + k // 2, dp_count), lax.rem(grp + k, 2)

    def loop(low, high, body):
        def step(k, carry):
            body(k)
            return carry

        lax.fori_loop(low, high, step, 0)

    barrier = pltpu.get_barrier_semaphore()

    def greet(k):
        peer_seq, peer_grp = peer(k)
        pl.semaphore_signal(
            barrier, inc=1, device_id=(dp, peer_seq, peer_grp), device_id_type=MESH_ID
        )

    def greet_first(k):
        peer_dp, peer_grp = first_peer(k)
        pl.semaphore_signal(
            barrier, inc=1, device_id=(peer_dp, seq, peer_grp), device_id_type=MESH_ID
        )

    loop(1, owner_count, greet)
    loop(2, 2 * dp_count, greet_first)

    gain_part[...] = jnp.zeros_like(gain_part)
    pl.semaphore_wait(barrier, owner_count - 1 + 2 * dp_count - 2)

    def remote(src, dst, send, recv, target):
        return pltpu.make_async_remote_copy(
            src_ref=src,
            dst_ref=dst,
            send_sem=send,
            recv_sem=recv,
            device_id=target,
            device_id_type=MESH_ID,
        )

    all_heads = pl.ds(0, heads)
    given = pl.ds(pl.multiple_of(other * heads, heads), heads)
    kept = pl.ds(pl.multiple_of(grp * heads, heads), heads)
    my_rows = pl.ds(pl.multiple_of(grp * image_rows, image_rows), image_rows)
    other_rows = pl.ds(pl.multiple_of(other * image_rows, image_rows), image_rows)
    partner = (dp, seq, other)
    remote(
        image_proj.at[:, 0, given],
        image_in.at[pl.ds(0, 3), all_heads, my_rows],
        image_send.at[0],
        image_recv.at[0],
        partner,
    ).start()
    remote(
        image_grad.at[0, given],
        image_in.at[3, all_heads, my_rows],
        image_send.at[1],
        image_recv.at[1],
        partner,
    ).start()
    local_images = (
        pltpu.make_async_copy(
            image_proj.at[:, 0, kept],
            image_in.at[pl.ds(0, 3), all_heads, my_rows],
            image_recv.at[2],
        ),
        pltpu.make_async_copy(
            image_grad.at[0, kept], image_in.at[3, all_heads, my_rows], image_recv.at[3]
        ),
    )
    for copy in local_images:
        copy.start()

    def text_step(step):
        own = pl.ds(step * hps, hps)

        def ends(peer_seq, peer_grp):
            theirs = pl.ds(peer_grp * heads + step * hps, hps)
            return (
                (text_proj.at[:, peer_seq, theirs], text_in.at[pl.ds(0, 3), own, me]),
                (text_grad.at[peer_seq, theirs], text_in.at[3, own, me]),
            )

        for i, (src, dst) in enumerate(ends(seq, grp)):
            pltpu.make_async_copy(src, dst, text_recv.at[i, step]).start()

        def send(k):
            peer_seq, peer_grp = peer(k)
            for i, (src, dst) in enumerate(ends(peer_seq, peer_grp)):
                remote(
                    src,
                    dst,
                    text_send.at[i, step],
                    text_recv.at[i, step],
                    (dp, peer_seq, peer_grp),
                ).start()

        loop(1, owner_count, send)

    loop(0, steps, text_step)

    for copy in local_images:
        copy.wait()
    for i, part in enumerate((image_in.at[pl.ds(0, 3), all_heads, other_rows], image_in.at[3, all_heads, other_rows])):
        pltpu.make_async_copy(part, part, image_recv.at[i]).wait()

    total = text_rows + 2 * image_rows
    place = lax.broadcasted_iota(jnp.int32, (1, total), 1)
    bias = jnp.where((place >= text_rows) | (place < length[0]), 0.0, -1.0)

    def work(step):
        own = pl.ds(step * hps, hps)
        for i, part in enumerate((text_in.at[pl.ds(0, 3), own], text_in.at[3, own])):
            pltpu.make_async_copy(part, part, text_recv.at[i, step]).wait()
        for j in range(hps):
            head = step * hps + j
            rows = [
                jnp.concatenate(
                    [
                        text_in[c, head].reshape(text_rows, text_in.shape[-1]),
                        image_in[c, head],
                    ],
                    axis=0,
                )
                for c in range(4)
            ]
            results, parts = attend_head(*rows, bias, gains, text_rows)
            gain_part[...] += parts
            for c, result in enumerate(results):
                text_res[c, head] = result[:text_rows].reshape(text_res.shape[2:])
                image_res[c, head] = result[text_rows:]

        def back_ends(owner):
            there = pl.ds(grp * heads + step * hps, hps)
            return (
                (text_res.at[0, own, owner], text_out.at[seq, there]),
                (text_res.at[pl.ds(1, 3), own, owner], text_proj_grad.at[:, seq, there]),
            )

        def send_back(k):
            peer_seq, peer_grp = peer(k)
            for i, (src, dst) in enumerate(back_ends(peer_seq * 2 + peer_grp)):
                remote(
                    src, dst, back_send.at[i], back_recv.at[i], (dp, peer_seq, peer_grp)
                ).start()

        loop(1, owner_count, send_back)
        for i, (src, dst) in enumerate(back_ends(me)):
            pltpu.make_async_copy(src, dst, back_recv.at[i]).start()

    loop(0, steps, work)

    remote(
        image_res.at[0, all_heads, other_rows],
        image_out.at[0, kept],
        image_back_send.at[0],
        image_back_recv.at[0],
        partner,
    ).start()
    remote(
        image_res.at[pl.ds(1, 3), all_heads, other_rows],
        image_proj_grad.at[:, 0, kept],
        image_back_send.at[1],
        image_back_recv.at[1],
        partner,
    ).start()
    local_results = (
        pltpu.make_async_copy(
            image_res.at[0, all_heads, my_rows], image_out.at[0, kept], image_back_recv.at[2]
        ),
        pltpu.make_async_copy(
            image_res.at[pl.ds(1, 3), all_heads, my_rows],
            image_proj_grad.at[:, 0, kept],
            image_back_recv.at[3],
        ),
    )
    for copy in local_results:
        copy.start()

    first_me = dp * 2 + grp
    gain_first[first_me] = gain_part[...]

    def send_first(k):
        peer_dp, peer_grp = first_peer(k)
        remote(
            gain_part,
            gain_first.at[first_me],
            gain_send.at[0],
            gain_recv.at[0],
            (peer_dp, seq, peer_grp),
        ).start()

    loop(1, 2 * dp_count, send_first)
    first_others = gain_first.at[pl.ds(0, 2 * dp_count - 1)]
    pltpu.make_async_copy(first_others, first_others, gain_recv.at[0]).wait()
    mid = jnp.sum(gain_first[...], axis=0)
    gain_mid[...] = mid
    gain_second[seq] = mid

    def send_second(k):
        remote(
            gain_mid,
            gain_second.at[seq],
            gain_send.at[1],
            gain_recv.at[1],
            (dp, seq_peer(k), grp),
        ).start()

    loop(1, seq_count, send_second)
    second_others = gain_second.at[pl.ds(0, seq_count - 1)]
    pltpu.make_async_copy(second_others, second_others, gain_recv.at[1]).wait()
    gain = jnp.sum(gain_second[...], axis=0) / samples
    gain_out[0] = gain[:2]
    gain_out[1] = gain[2:]

    for copy in local_results:
        copy.wait()
    sent = (
        (image_in.at[pl.ds(0, 3), all_heads, my_rows], image_send.at[0]),
        (image_in.at[3, all_heads, my_rows], image_send.at[1]),
        (image_out.at[0, kept], image_back_send.at[0]),
        (image_proj_grad.at[:, 0, kept], image_back_send.at[1]),
        (image_out.at[0, given], image_back_recv.at[0]),
        (image_proj_grad.at[:, 0, given], image_back_recv.at[1]),
        (first_others, gain_send.at[0]),
        (second_others, gain_send.at[1]),
        (text_out, back_recv.at[0]),
        (text_proj_grad, back_recv.at[1]),
        (text_res.at[0, :, pl.ds(0, owner_count - 1)], back_send.at[0]),
        (text_res.at[pl.ds(1, 3), :, pl.ds(0, owner_count - 1)], back_send.at[1]),
    )
    for part, semaphore in sent:
        pltpu.make_async_copy(part, part, semaphore).wait()

    def sent_text(step):
        own = pl.ds(step * hps, hps)
        others = pl.ds(0, owner_count - 1)
        for i, part in enumerate((text_in.at[pl.ds(0, 3), own, others], text_in.at[3, own, others])):
            pltpu.make_async_copy(part, part, text_send.at[i, step]).wait()

    loop(0, steps, sent_text)


def per_device(sizes, text_proj, image_proj, text_grad, image_grad, text_lengths, norm_gains):
    dp_count, seq_count, _ = sizes
    _, _, head_count, text_group, size = text_proj.shape
    image_rows = image_proj.shape[3]
    heads = head_count // 2
    owners = seq_count * 2
    steps = heads // HEADS_PER_STEP
    bf16 = jnp.bfloat16
    anywhere = pl.BlockSpec(memory_space=pl.ANY)
    text_shape = (4, heads, owners, text_group, size)
    image_shape = (4, heads, 2 * image_rows, size)
    dma = pltpu.SemaphoreType.DMA
    total = owners * text_group + 2 * image_rows
    text_out, text_proj_grad, image_out, image_proj_grad, gain_grad = pl.pallas_call(
        functools.partial(kernel, sizes),
        out_shape=(
            jax.ShapeDtypeStruct(text_grad.shape, bf16),
            jax.ShapeDtypeStruct(text_proj.shape, bf16),
            jax.ShapeDtypeStruct(image_grad.shape, bf16),
            jax.ShapeDtypeStruct(image_proj.shape, bf16),
            jax.ShapeDtypeStruct(norm_gains.shape, jnp.float32),
        ),
        in_specs=[anywhere] * 4
        + [pl.BlockSpec(memory_space=pltpu.SMEM), pl.BlockSpec(memory_space=pltpu.VMEM)],
        out_specs=(anywhere,) * 4 + (pl.BlockSpec(memory_space=pltpu.VMEM),),
        scratch_shapes=[
            pltpu.VMEM(text_shape, bf16),
            pltpu.VMEM(image_shape, bf16),
            pltpu.VMEM(text_shape, bf16),
            pltpu.VMEM(image_shape, bf16),
            pltpu.VMEM((4, size), jnp.float32),
            pltpu.VMEM((2 * dp_count, 4, size), jnp.float32),
            pltpu.VMEM((4, size), jnp.float32),
            pltpu.VMEM((seq_count, 4, size), jnp.float32),
            dma((2, steps)),
            dma((2, steps)),
            dma((2,)),
            dma((4,)),
            dma((2,)),
            dma((2,)),
            dma((2,)),
            dma((4,)),
            dma((2,)),
            dma((2,)),
        ],
        compiler_params=pltpu.CompilerParams(
            collective_id=0, has_side_effects=True, vmem_limit_bytes=40 << 20
        ),
        cost_estimate=pl.CostEstimate(
            flops=heads * 12 * total * total * size,
            bytes_accessed=2 * 8 * heads * total * size * 2,
            transcendentals=heads * total * total,
        ),
    )(text_proj, text_grad, image_proj, image_grad, text_lengths, norm_gains)
    return text_out, image_out, text_proj_grad, image_proj_grad, gain_grad


def solution(mesh):
    dp_count, seq_count = mesh.shape["dp"], mesh.shape["seq"]
    text_proj = P(None, "dp", None, ("seq", "grp"), None)
    image_proj = P(None, ("dp", "seq"), None, "grp", None)
    text_grad = P("dp", None, ("seq", "grp"), None)
    image_grad = P(("dp", "seq"), None, "grp", None)

    def run(*args):
        sizes = (dp_count, seq_count, args[4].shape[0])
        return jax.shard_map(
            functools.partial(per_device, sizes),
            mesh=mesh,
            in_specs=(text_proj, image_proj, text_grad, image_grad, P(("dp", "seq")), P()),
            out_specs=(text_grad, image_grad, text_proj, image_proj, P()),
            check_vma=False,
        )(*args)

    return run
```

time: 207 us -> 95.4 us (0.46)
  blocking collectives: 105 us -> 0 us
  Pallas kernels: 0 us -> 85.5 us
  starting transfers between devices: 29.6 us -> 0 us
  waiting for transfers between devices: 28.6 us -> 0 us
  matrix products: 20.6 us -> 0 us
  other arithmetic: 8.04 us -> 0 us
  local copies, waits for them, and re-layouts: 12.9 us -> 8.35 us
    pallas_call x0 -> x1, Pallas kernels: none -> 85.5 us  [per_device(): pl.pallas_call(functools.partial(kernel, sizes), out_shape=(jax.ShapeDtyp...]
    psum x5 -> x0, blocking collectives: 59 us -> none  [one_axis_at_a_time(): return functools.reduce(lax.psum, axes, shard)]
    all_to_all x3 -> x0, blocking collectives: 45.9 us -> none  [the longest x1 31.9 us: cut_exchange(): lax.all_to_all(share, axis, split_axis=0, concat_axis=0, tiled=True)]
    all_to_all x2 -> x0, starting transfers between devices: 29.6 us -> none  [the longest x1 20.7 us: in_one_piece(): lax.all_to_all(both, axis, split_axis=split_dim, concat_axis=concat_dim,...]
    all_to_all x2 -> x0, waiting for transfers between devices: 28.6 us -> none  [the longest x1 17.9 us: in_one_piece(): lax.all_to_all(both, axis, split_axis=split_dim, concat_axis=concat_dim,...]
    dot_general x36 -> x0, matrix products: 20.6 us -> none  [the longest x6 5.47 us: backward_terms(): jnp.einsum('nqk,nkd->nqd', grad_scores, key_rows, preferred_element_type=...]
    unnamed x14 -> x15, local copies, waits for them, and re-layouts: 3.11 us -> 8.35 us
    slice x15 -> x0, local copies, waits for them, and re-layouts: 3.73 us -> none  [the longest x6 1.47 us: in_one_piece(): gathered.append(lax.slice_in_dim(out, at, at + a.shape[along], axis=along))]
  transfers between devices with their start and end apart: 2 -> 0, of which waited for: 2 -> 0; matrix products, arithmetic and copies ran while one was open for 2% -> 0% of each run, Pallas kernels for 0% -> 0%
where the time goes in v1:
time: 95.4 us; the launch traced here: 95.1 us
  Pallas kernels  85.5 us (90%)
  local copies, waits for them, and re-layouts  8.35 us (9%)
  between operations  1.3 us (1%)
    pallas_call x1, Pallas kernels, per_device(): pl.pallas_call(functools.partial(kernel, sizes), out_shape=(jax.ShapeDtyp...  85.5 us
    unnamed x15, local copies, waits for them, and re-layouts  8.35 us

profile of v1, /device:TPU:1, one launch (start us, length us, event | category | flops | bytes accessed | tf_op | source)
XLA Modules:
  0.0 95.1 jit_solution(12864425804243270603)
XLA Ops:
  1.3 0.0 copy-start
  1.3 1.1 %copy-done = bf16[3,1,12,80,128]{4,3,2,1,0:T(8,128)(2,1)S(1)} copy-done((bf16[3,1,12,80,128]{4,3,2,1,0:T(8,128)(2,1)S(1)}, bf16[3,1,12,80,128]{4,3,2,1,0:T(8,128)(2,1)}, u32[]{:S(2)}) %copy-start) | copy-done | bytes 737304
  2.4 0.0 copy-start.1
  2.4 1.1 %copy-done.1 = bf16[3,32,12,2,128]{4,3,2,1,0:T(2,128)(2,1)S(1)} copy-done((bf16[3,32,12,2,128]{4,3,2,1,0:T(2,128)(2,1)S(1)}, bf16[3,32,12,2,128]{4,3,2,1,0:T(2,128)(2,1)}, u32[]{:S(2)}) %copy-start.1) | copy-done | bytes 589848
  3.5 0.0 copy-start.2
  3.5 0.9 copy-done.2
  4.4 0.0 copy-start.3
  4.4 0.9 copy-done.3
  5.3 0.0 copy-start.4
  5.3 0.7 copy-done.4
  6.0 85.5 %shard_map.101 = (bf16[32,12,2,128]{3,2,1,0:T(2,128)(2,1)S(1)}, bf16[3,32,12,2,128]{4,3,2,1,0:T(2,128)(2,1)S(1)}, bf16[1,12,80,128]{3,2,1,0:T(8,128)(2,1)S(1)}, ...) custom-call(bf16[3,32,12,2,128]{4,3,2,1,0:T(2,128)(2,1)S(1)} %copy-done.1, ...), custom_call_target="tpu_custom_call" | custom-call | flops 764411904 | bytes 7077888 | tf_op jit(solution)/shard_map/pallas_call | solution.py:385
  91.5 0.7 copy.17
  92.2 0.7 copy.18
  92.9 0.8 copy.19
  93.7 0.9 copy.20
  94.5 0.6 copy.21
Async XLA Ops:
  1.3 1.1 %copy-start = (bf16[3,1,12,80,128]{4,3,2,1,0:T(8,128)(2,1)S(1)}, bf16[3,1,12,80,128]{4,3,2,1,0:T(8,128)(2,1)}, u32[]{:S(2)}) copy-start(bf16[3,1,12,80,128]{4,3,2,1,0:T(8,128)(2,1)} %image_proj.1) | copy-start | bytes 2211844
  2.4 1.1 %copy-start.1 = (bf16[3,32,12,2,128]{4,3,2,1,0:T(2,128)(2,1)S(1)}, bf16[3,32,12,2,128]{4,3,2,1,0:T(2,128)(2,1)}, u32[]{:S(2)}) copy-start(bf16[3,32,12,2,128]{4,3,2,1,0:T(2,128)(2,1)} %text_proj.1) | copy-start | bytes 1769476
  3.5 0.9 copy-start.2
  4.4 0.9 copy-start.3
  5.3 0.7 copy-start.4

commit v2 on v1

--- a/solution.py
+++ b/solution.py
@@ -11,7 +11,11 @@
 MASKED = -1e30
 MESH_ID = pl.DeviceIdType.MESH
 NZ = 4
-HEADS_PER_STEP = 2
+HEADS_PER_STEP = 1
+VMEM_LIMIT = 60 << 20
+HELD = 3
+TURN = 11
+STRIDE = 29
 
 
 def dot(a, b, contract_a, contract_b):
@@ -80,8 +84,8 @@
     text_grad,
     image_proj,
     image_grad,
-    length,
-    gains,
+    length_any,
+    gains_any,
     text_out,
     text_proj_grad,
     image_out,
@@ -95,6 +99,8 @@
     gain_first,
     gain_mid,
     gain_second,
+    length,
+    gains,
     text_send,
     text_recv,
     image_send,
@@ -105,6 +111,7 @@
     image_back_recv,
     gain_send,
     gain_recv,
+    small_recv,
 ):
     dp_count, seq_count, samples = sizes
     rows_y = seq_count // NZ
@@ -117,14 +124,19 @@
     image_rows = image_proj.shape[3]
     hps = HEADS_PER_STEP
     steps = heads // hps
+    held = min(HELD, steps - 1)
+
+    way = 1 - 2 * grp
 
     def seq_peer(k):
-        y = lax.rem(seq // NZ + k // NZ, rows_y)
-        z = lax.rem(lax.rem(seq, NZ) + lax.rem(k, NZ), NZ)
+        y = lax.rem(seq // NZ + way * (k // NZ) + rows_y, rows_y)
+        z = lax.rem(lax.rem(seq, NZ) + way * lax.rem(k, NZ) + NZ, NZ)
         return y * NZ + z
 
     def peer(k):
-        return seq_peer(lax.rem(k, seq_count)), lax.rem(grp + k // seq_count, 2)
+        turned = lax.rem(k - 1 + seq * TURN, owner_count - 1) + 1
+        place = lax.rem(turned * STRIDE, owner_count)
+        return seq_peer(place // 2), lax.rem(grp + place, 2)
 
     def first_peer(k):
         return lax.rem(dp + k // 2, dp_count), lax.rem(grp + k, 2)
@@ -153,6 +165,43 @@
     loop(1, owner_count, greet)
     loop(2, 2 * dp_count, greet_first)
 
+    all_heads = pl.ds(0, heads)
+    given = pl.ds(pl.multiple_of(other * heads, heads), heads)
+    kept = pl.ds(pl.multiple_of(grp * heads, heads), heads)
+    my_rows = pl.ds(pl.multiple_of(grp * image_rows, image_rows), image_rows)
+    other_rows = pl.ds(pl.multiple_of(other * image_rows, image_rows), image_rows)
+    local_images = (
+        pltpu.make_async_copy(
+            image_proj.at[:, 0, kept],
+            image_in.at[pl.ds(0, 3), all_heads, my_rows],
+            image_recv.at[2],
+        ),
+        pltpu.make_async_copy(
+            image_grad.at[0, kept], image_in.at[3, all_heads, my_rows], image_recv.at[3]
+        ),
+    )
+    for copy in local_images:
+        copy.start()
+    small = (
+        pltpu.make_async_copy(length_any, length, small_recv.at[0]),
+        pltpu.make_async_copy(gains_any, gains, small_recv.at[1]),
+    )
+    for copy in small:
+        copy.start()
+
+    def text_ends(step, peer_seq, peer_grp):
+        own = pl.ds(step * hps, hps)
+        theirs = pl.ds(peer_grp * heads + step * hps, hps)
+        return (
+            (text_proj.at[:, peer_seq, theirs], text_in.at[pl.ds(0, 3), own, me]),
+            (text_grad.at[peer_seq, theirs], text_in.at[3, own, me]),
+        )
+
+    def text_stays(step):
+        for i, (src, dst) in enumerate(text_ends(step, seq, grp)):
+            pltpu.make_async_copy(src, dst, text_recv.at[i, step]).start()
+
+    loop(0, steps, text_stays)
     gain_part[...] = jnp.zeros_like(gain_part)
     pl.semaphore_wait(barrier, owner_count - 1 + 2 * dp_count - 2)
 
@@ -166,11 +215,6 @@
             device_id_type=MESH_ID,
         )
 
-    all_heads = pl.ds(0, heads)
-    given = pl.ds(pl.multiple_of(other * heads, heads), heads)
-    kept = pl.ds(pl.multiple_of(grp * heads, heads), heads)
-    my_rows = pl.ds(pl.multiple_of(grp * image_rows, image_rows), image_rows)
-    other_rows = pl.ds(pl.multiple_of(other * image_rows, image_rows), image_rows)
     partner = (dp, seq, other)
     remote(
         image_proj.at[:, 0, given],
@@ -186,35 +230,10 @@
         image_recv.at[1],
         partner,
     ).start()
-    local_images = (
-        pltpu.make_async_copy(
-            image_proj.at[:, 0, kept],
-            image_in.at[pl.ds(0, 3), all_heads, my_rows],
-            image_recv.at[2],
-        ),
-        pltpu.make_async_copy(
-            image_grad.at[0, kept], image_in.at[3, all_heads, my_rows], image_recv.at[3]
-        ),
-    )
-    for copy in local_images:
-        copy.start()
-
     def text_step(step):
-        own = pl.ds(step * hps, hps)
-
-        def ends(peer_seq, peer_grp):
-            theirs = pl.ds(peer_grp * heads + step * hps, hps)
-            return (
-                (text_proj.at[:, peer_seq, theirs], text_in.at[pl.ds(0, 3), own, me]),
-                (text_grad.at[peer_seq, theirs], text_in.at[3, own, me]),
-            )
-
-        for i, (src, dst) in enumerate(ends(seq, grp)):
-            pltpu.make_async_copy(src, dst, text_recv.at[i, step]).start()
-
         def send(k):
             peer_seq, peer_grp = peer(k)
-            for i, (src, dst) in enumerate(ends(peer_seq, peer_grp)):
+            for i, (src, dst) in enumerate(text_ends(step, peer_seq, peer_grp)):
                 remote(
                     src,
                     dst,
@@ -227,7 +246,7 @@
 
     loop(0, steps, text_step)
 
-    for copy in local_images:
+    for copy in local_images + small:
         copy.wait()
     for i, part in enumerate((image_in.at[pl.ds(0, 3), all_heads, other_rows], image_in.at[3, all_heads, other_rows])):
         pltpu.make_async_copy(part, part, image_recv.at[i]).wait()
@@ -235,6 +254,63 @@
     total = text_rows + 2 * image_rows
     place = lax.broadcasted_iota(jnp.int32, (1, total), 1)
     bias = jnp.where((place >= text_rows) | (place < length[0]), 0.0, -1.0)
+
+    first_me = dp * 2 + grp
+    first_others = gain_first.at[pl.ds(0, 2 * dp_count - 1)]
+    second_others = gain_second.at[pl.ds(0, seq_count - 1)]
+
+    def gain_hop_one():
+        gain_first[first_me] = gain_part[...]
+
+        def send_first(k):
+            peer_dp, peer_grp = first_peer(k)
+            remote(
+                gain_part,
+                gain_first.at[first_me],
+                gain_send.at[0],
+                gain_recv.at[0],
+                (peer_dp, seq, peer_grp),
+            ).start()
+
+        loop(1, 2 * dp_count, send_first)
+
+    def gain_hop_two():
+        pltpu.make_async_copy(first_others, first_others, gain_recv.at[0]).wait()
+        mid = jnp.sum(gain_first[...], axis=0)
+        gain_mid[...] = mid
+        gain_second[seq] = mid
+
+        def send_second(k):
+            remote(
+                gain_mid,
+                gain_second.at[seq],
+                gain_send.at[1],
+                gain_recv.at[1],
+                (dp, seq_peer(k), grp),
+            ).start()
+
+        loop(1, seq_count, send_second)
+
+    def give_back(step):
+        own = pl.ds(step * hps, hps)
+        there = pl.ds(grp * heads + step * hps, hps)
+
+        def back_ends(owner):
+            return (
+                (text_res.at[0, own, owner], text_out.at[seq, there]),
+                (text_res.at[pl.ds(1, 3), own, owner], text_proj_grad.at[:, seq, there]),
+            )
+
+        def send_back(k):
+            peer_seq, peer_grp = peer(k)
+            for i, (src, dst) in enumerate(back_ends(peer_seq * 2 + peer_grp)):
+                remote(
+                    src, dst, back_send.at[i], back_recv.at[i], (dp, peer_seq, peer_grp)
+                ).start()
+
+        loop(1, owner_count, send_back)
+        for i, (src, dst) in enumerate(back_ends(me)):
+            pltpu.make_async_copy(src, dst, back_recv.at[i]).start()
 
     def work(step):
         own = pl.ds(step * hps, hps)
@@ -257,26 +333,13 @@
             for c, result in enumerate(results):
                 text_res[c, head] = result[:text_rows].reshape(text_res.shape[2:])
                 image_res[c, head] = result[text_rows:]
-
-        def back_ends(owner):
-            there = pl.ds(grp * heads + step * hps, hps)
-            return (
-                (text_res.at[0, own, owner], text_out.at[seq, there]),
-                (text_res.at[pl.ds(1, 3), own, owner], text_proj_grad.at[:, seq, there]),
-            )
-
-        def send_back(k):
-            peer_seq, peer_grp = peer(k)
-            for i, (src, dst) in enumerate(back_ends(peer_seq * 2 + peer_grp)):
-                remote(
-                    src, dst, back_send.at[i], back_recv.at[i], (dp, peer_seq, peer_grp)
-                ).start()
-
-        loop(1, owner_count, send_back)
-        for i, (src, dst) in enumerate(back_ends(me)):
-            pltpu.make_async_copy(src, dst, back_recv.at[i]).start()
+        pl.when(step < held)(lambda: give_back(step))
 
     loop(0, steps, work)
+    gain_hop_one()
+    loop(held, steps - 1, give_back)
+    gain_hop_two()
+    loop(steps - 1, steps, give_back)
 
     remote(
         image_res.at[0, all_heads, other_rows],
@@ -305,37 +368,6 @@
     for copy in local_results:
         copy.start()
 
-    first_me = dp * 2 + grp
-    gain_first[first_me] = gain_part[...]
-
-    def send_first(k):
-        peer_dp, peer_grp = first_peer(k)
-        remote(
-            gain_part,
-            gain_first.at[first_me],
-            gain_send.at[0],
-            gain_recv.at[0],
-            (peer_dp, seq, peer_grp),
-        ).start()
-
-    loop(1, 2 * dp_count, send_first)
-    first_others = gain_first.at[pl.ds(0, 2 * dp_count - 1)]
-    pltpu.make_async_copy(first_others, first_others, gain_recv.at[0]).wait()
-    mid = jnp.sum(gain_first[...], axis=0)
-    gain_mid[...] = mid
-    gain_second[seq] = mid
-
-    def send_second(k):
-        remote(
-            gain_mid,
-            gain_second.at[seq],
-            gain_send.at[1],
-            gain_recv.at[1],
-            (dp, seq_peer(k), grp),
-        ).start()
-
-    loop(1, seq_count, send_second)
-    second_others = gain_second.at[pl.ds(0, seq_count - 1)]
     pltpu.make_async_copy(second_others, second_others, gain_recv.at[1]).wait()
     gain = jnp.sum(gain_second[...], axis=0) / samples
     gain_out[0] = gain[:2]
@@ -369,6 +401,22 @@
     loop(0, steps, sent_text)
 
 
+def put_out(count, *refs):
+    results, outs, held = refs[:count], refs[count : 2 * count], refs[2 * count : 3 * count]
+    semaphores = refs[-1]
+    reads = [
+        pltpu.make_async_copy(results[i], held[i], semaphores.at[0, i]) for i in range(count)
+    ]
+    writes = [pltpu.make_async_copy(held[i], outs[i], semaphores.at[1, i]) for i in range(count)]
+    for copy in reads:
+        copy.start()
+    for read, write in zip(reads, writes):
+        read.wait()
+        write.start()
+    for copy in writes:
+        copy.wait()
+
+
 def per_device(sizes, text_proj, image_proj, text_grad, image_grad, text_lengths, norm_gains):
     dp_count, seq_count, _ = sizes
     _, _, head_count, text_group, size = text_proj.shape
@@ -382,7 +430,7 @@
     image_shape = (4, heads, 2 * image_rows, size)
     dma = pltpu.SemaphoreType.DMA
     total = owners * text_group + 2 * image_rows
-    text_out, text_proj_grad, image_out, image_proj_grad, gain_grad = pl.pallas_call(
+    results = pl.pallas_call(
         functools.partial(kernel, sizes),
         out_shape=(
             jax.ShapeDtypeStruct(text_grad.shape, bf16),
@@ -391,8 +439,7 @@
             jax.ShapeDtypeStruct(image_proj.shape, bf16),
             jax.ShapeDtypeStruct(norm_gains.shape, jnp.float32),
         ),
-        in_specs=[anywhere] * 4
-        + [pl.BlockSpec(memory_space=pltpu.SMEM), pl.BlockSpec(memory_space=pltpu.VMEM)],
+        in_specs=[anywhere] * 6,
         out_specs=(anywhere,) * 4 + (pl.BlockSpec(memory_space=pltpu.VMEM),),
         scratch_shapes=[
             pltpu.VMEM(text_shape, bf16),
@@ -403,6 +450,8 @@
             pltpu.VMEM((2 * dp_count, 4, size), jnp.float32),
             pltpu.VMEM((4, size), jnp.float32),
             pltpu.VMEM((seq_count, 4, size), jnp.float32),
+            pltpu.SMEM((1,), jnp.int32),
+            pltpu.VMEM(norm_gains.shape, jnp.float32),
             dma((2, steps)),
             dma((2, steps)),
             dma((2,)),
@@ -413,9 +462,10 @@
             dma((4,)),
             dma((2,)),
             dma((2,)),
+            dma((2,)),
         ],
         compiler_params=pltpu.CompilerParams(
-            collective_id=0, has_side_effects=True, vmem_limit_bytes=40 << 20
+            collective_id=0, has_side_effects=True, vmem_limit_bytes=VMEM_LIMIT
         ),
         cost_estimate=pl.CostEstimate(
             flops=heads * 12 * total * total * size,
@@ -423,6 +473,14 @@
             transcendentals=heads * total * total,
         ),
     )(text_proj, text_grad, image_proj, image_grad, text_lengths, norm_gains)
+    text_out, text_proj_grad, image_out, image_proj_grad, gain_grad = pl.pallas_call(
+        functools.partial(put_out, len(results)),
+        out_shape=tuple(jax.ShapeDtypeStruct(r.shape, r.dtype) for r in results),
+        in_specs=[anywhere] * len(results),
+        out_specs=(anywhere,) * len(results),
+        scratch_shapes=[pltpu.VMEM(r.shape, r.dtype) for r in results] + [dma((2, len(results)))],
+        compiler_params=pltpu.CompilerParams(vmem_limit_bytes=VMEM_LIMIT),
+    )(*results)
     return text_out, image_out, text_proj_grad, image_proj_grad, gain_grad
 
 

time: 95.4 us -> 88.8 us (0.931)
  local copies, waits for them, and re-layouts: 8.35 us -> 0 us
  Pallas kernels: 85.5 us -> 87.4 us
    unnamed x15 -> x0, local copies, waits for them, and re-layouts: 8.35 us -> none
    pallas_call x0 -> x1, Pallas kernels: none -> 2.43 us  [per_device(): pl.pallas_call(functools.partial(put_out, len(results)), out_shape=tuple(...]
where the time goes in v2:
time: 88.8 us; the launch traced here: 88.7 us
  Pallas kernels  87.4 us (98%)
  between operations  1.29 us (1%)
    pallas_call x1, Pallas kernels, per_device(): pl.pallas_call(functools.partial(kernel, sizes), out_shape=(jax.ShapeDtyp...  85 us
    pallas_call x1, Pallas kernels, per_device(): pl.pallas_call(functools.partial(put_out, len(results)), out_shape=tuple(...  2.43 us

profile of v2, /device:TPU:1, one launch (start us, length us, event | category | flops | bytes accessed | tf_op | source)
XLA Modules:
  0.0 88.7 jit_solution(3693103408622244152)
XLA Ops:
  1.3 85.0 %shard_map.101 = (bf16[32,12,2,128]{3,2,1,0:T(2,128)(2,1)}, bf16[3,32,12,2,128]{4,3,2,1,0:T(2,128)(2,1)}, bf16[1,12,80,128]{3,2,1,0:T(8,128)(2,1)}, bf16[3,1,12,80,128]{4,3,2,1,0:T(8,128)(2,1)}, f32[2,2,128]{2,1,0:T(2,128)}) custom-call(bf16[3,32,12,2,128]{4,3,2,1,0:T(2,128)(2,1)} %text_proj.1, bf16[32,12,2,128]{3,2,1,0:T(2,128)(2,1)} %text_grad.1, ...), custom_call_target="tpu_custom_call" | custom-call | flops 764411904 | bytes 7077888 | tf_op jit(solution)/shard_map/pallas_call | solution.py:433
  86.2 2.4 %shard_map.102 = (bf16[32,12,2,128]{3,2,1,0:T(2,128)(2,1)}, bf16[3,32,12,2,128]{4,3,2,1,0:T(2,128)(2,1)}, bf16[1,12,80,128]{3,2,1,0:T(8,128)(2,1)}, bf16[3,1,12,80,128]{4,3,2,1,0:T(8,128)(2,1)}, f32[2,2,128]{2,1,0:T(2,128)}) custom-call(bf16[32,12,2,128]{3,2,1,0:T(2,128)(2,1)} %get-tuple-element.15.refs_0_, ...), custom_call_target="tpu_custom_call" | custom-call | tf_op jit(solution)/shard_map/pallas_call | solution.py:476

commit v3 on v2

--- a/solution.py
+++ b/solution.py
@@ -11,9 +11,10 @@
 MASKED = -1e30
 MESH_ID = pl.DeviceIdType.MESH
 NZ = 4
-HEADS_PER_STEP = 1
+HEADS_PER_STEP = 2
 VMEM_LIMIT = 60 << 20
-HELD = 3
+HELD = 1
+THIRD_AFTER = 40
 TURN = 11
 STRIDE = 29
 
@@ -99,6 +100,8 @@
     gain_first,
     gain_mid,
     gain_second,
+    gain_late,
+    gain_third,
     length,
     gains,
     text_send,
@@ -257,7 +260,9 @@
 
     first_me = dp * 2 + grp
     first_others = gain_first.at[pl.ds(0, 2 * dp_count - 1)]
-    second_others = gain_second.at[pl.ds(0, seq_count - 1)]
+    second_others = gain_second.at[pl.ds(0, rows_y - 1)]
+    third_others = gain_third.at[pl.ds(0, NZ - 1)]
+    my_y, my_z = seq // NZ, lax.rem(seq, NZ)
 
     def gain_hop_one():
         gain_first[first_me] = gain_part[...]
@@ -278,20 +283,37 @@
         pltpu.make_async_copy(first_others, first_others, gain_recv.at[0]).wait()
         mid = jnp.sum(gain_first[...], axis=0)
         gain_mid[...] = mid
-        gain_second[seq] = mid
+        gain_second[my_y] = mid
 
         def send_second(k):
             remote(
                 gain_mid,
-                gain_second.at[seq],
+                gain_second.at[my_y],
                 gain_send.at[1],
                 gain_recv.at[1],
+                (dp, seq_peer(k * NZ), grp),
+            ).start()
+
+        loop(1, rows_y, send_second)
+
+    def gain_hop_three():
+        pltpu.make_async_copy(second_others, second_others, gain_recv.at[1]).wait()
+        late = jnp.sum(gain_second[...], axis=0)
+        gain_late[...] = late
+        gain_third[my_z] = late
+
+        def send_third(k):
+            remote(
+                gain_late,
+                gain_third.at[my_z],
+                gain_send.at[2],
+                gain_recv.at[2],
                 (dp, seq_peer(k), grp),
             ).start()
 
-        loop(1, seq_count, send_second)
-
-    def give_back(step):
+        loop(1, NZ, send_third)
+
+    def give_back(step, low=1, high=owner_count):
         own = pl.ds(step * hps, hps)
         there = pl.ds(grp * heads + step * hps, hps)
 
@@ -308,9 +330,10 @@
                     src, dst, back_send.at[i], back_recv.at[i], (dp, peer_seq, peer_grp)
                 ).start()
 
-        loop(1, owner_count, send_back)
-        for i, (src, dst) in enumerate(back_ends(me)):
-            pltpu.make_async_copy(src, dst, back_recv.at[i]).start()
+        loop(low, high, send_back)
+        if low == 1:
+            for i, (src, dst) in enumerate(back_ends(me)):
+                pltpu.make_async_copy(src, dst, back_recv.at[i]).start()
 
     def work(step):
         own = pl.ds(step * hps, hps)
@@ -339,7 +362,10 @@
     gain_hop_one()
     loop(held, steps - 1, give_back)
     gain_hop_two()
-    loop(steps - 1, steps, give_back)
+    third_after = min(THIRD_AFTER, owner_count)
+    give_back(steps - 1, 1, third_after)
+    gain_hop_three()
+    give_back(steps - 1, third_after, owner_count)
 
     remote(
         image_res.at[0, all_heads, other_rows],
@@ -368,8 +394,8 @@
     for copy in local_results:
         copy.start()
 
-    pltpu.make_async_copy(second_others, second_others, gain_recv.at[1]).wait()
-    gain = jnp.sum(gain_second[...], axis=0) / samples
+    pltpu.make_async_copy(third_others, third_others, gain_recv.at[2]).wait()
+    gain = jnp.sum(gain_third[...], axis=0) / samples
     gain_out[0] = gain[:2]
     gain_out[1] = gain[2:]
 
@@ -384,6 +410,7 @@
         (image_proj_grad.at[:, 0, given], image_back_recv.at[1]),
         (first_others, gain_send.at[0]),
         (second_others, gain_send.at[1]),
+        (third_others, gain_send.at[2]),
         (text_out, back_recv.at[0]),
         (text_proj_grad, back_recv.at[1]),
         (text_res.at[0, :, pl.ds(0, owner_count - 1)], back_send.at[0]),
@@ -449,7 +476,9 @@
             pltpu.VMEM((4, size), jnp.float32),
             pltpu.VMEM((2 * dp_count, 4, size), jnp.float32),
             pltpu.VMEM((4, size), jnp.float32),
-            pltpu.VMEM((seq_count, 4, size), jnp.float32),
+            pltpu.VMEM((seq_count // NZ, 4, size), jnp.float32),
+            pltpu.VMEM((4, size), jnp.float32),
+            pltpu.VMEM((NZ, 4, size), jnp.float32),
             pltpu.SMEM((1,), jnp.int32),
             pltpu.VMEM(norm_gains.shape, jnp.float32),
             dma((2, steps)),
@@ -460,8 +489,8 @@
             dma((2,)),
             dma((2,)),
             dma((4,)),
-            dma((2,)),
-            dma((2,)),
+            dma((3,)),
+            dma((3,)),
             dma((2,)),
         ],
         compiler_params=pltpu.CompilerParams(

time: 88.8 us -> 90 us (1.014)
  Pallas kernels: 87.4 us -> 88.6 us
    pallas_call x1, Pallas kernels: 85 us -> 86.1 us  [per_device(): pl.pallas_call(functools.partial(kernel, sizes), out_shape=(jax.ShapeDtyp...]
where the time goes in v3:
time: 90 us; the launch traced here: 89.9 us
  Pallas kernels  88.6 us (98%)
  between operations  1.29 us (1%)
    pallas_call x1, Pallas kernels, per_device(): pl.pallas_call(functools.partial(kernel, sizes), out_shape=(jax.ShapeDtyp...  86.1 us
    pallas_call x1, Pallas kernels, per_device(): pl.pallas_call(functools.partial(put_out, len(results)), out_shape=tuple(...  2.43 us

profile of v3, /device:TPU:1, one launch (start us, length us, event | category | flops | bytes accessed | tf_op | source)
XLA Modules:
  0.0 89.9 jit_solution(15998048054516318331)
XLA Ops:
  1.3 86.1 %shard_map.101 = (bf16[32,12,2,128]{3,2,1,0:T(2,128)(2,1)}, bf16[3,32,12,2,128]{4,3,2,1,0:T(2,128)(2,1)}, bf16[1,12,80,128]{3,2,1,0:T(8,128)(2,1)}, bf16[3,1,12,80,128]{4,3,2,1,0:T(8,128)(2,1)}, f32[2,2,128]{2,1,0:T(2,128)}) custom-call(bf16[3,32,12,2,128]{4,3,2,1,0:T(2,128)(2,1)} %text_proj.1, bf16[32,12,2,128]{3,2,1,0:T(2,128)(2,1)} %text_grad.1, ...), custom_call_target="tpu_custom_call" | custom-call | flops 764411904 | bytes 7077888 | tf_op jit(solution)/shard_map/pallas_call | solution.py:460
  87.4 2.4 %shard_map.102 = (bf16[32,12,2,128]{3,2,1,0:T(2,128)(2,1)}, bf16[3,32,12,2,128]{4,3,2,1,0:T(2,128)(2,1)}, bf16[1,12,80,128]{3,2,1,0:T(8,128)(2,1)}, bf16[3,1,12,80,128]{4,3,2,1,0:T(8,128)(2,1)}, f32[2,2,128]{2,1,0:T(2,128)}) custom-call(bf16[32,12,2,128]{3,2,1,0:T(2,128)(2,1)} %get-tuple-element.15.refs_0_, ...), custom_call_target="tpu_custom_call" | custom-call | tf_op jit(solution)/shard_map/pallas_call | solution.py:505

commit v4 on v3

--- a/solution.py
+++ b/solution.py
@@ -13,6 +13,7 @@
 NZ = 4
 HEADS_PER_STEP = 2
 VMEM_LIMIT = 60 << 20
+PIECES = 4
 HELD = 1
 THIRD_AFTER = 40
 TURN = 11
@@ -218,6 +219,22 @@
             device_id_type=MESH_ID,
         )
 
+    def text_step(step):
+        def send(k):
+            peer_seq, peer_grp = peer(k)
+            for i, (src, dst) in enumerate(text_ends(step, peer_seq, peer_grp)):
+                remote(
+                    src,
+                    dst,
+                    text_send.at[i, step],
+                    text_recv.at[i, step],
+                    (dp, peer_seq, peer_grp),
+                ).start()
+
+        loop(1, owner_count, send)
+
+    loop(0, 1, text_step)
+
     partner = (dp, seq, other)
     remote(
         image_proj.at[:, 0, given],
@@ -233,21 +250,7 @@
         image_recv.at[1],
         partner,
     ).start()
-    def text_step(step):
-        def send(k):
-            peer_seq, peer_grp = peer(k)
-            for i, (src, dst) in enumerate(text_ends(step, peer_seq, peer_grp)):
-                remote(
-                    src,
-                    dst,
-                    text_send.at[i, step],
-                    text_recv.at[i, step],
-                    (dp, peer_seq, peer_grp),
-                ).start()
-
-        loop(1, owner_count, send)
-
-    loop(0, steps, text_step)
+    loop(1, steps, text_step)
 
     for copy in local_images + small:
         copy.wait()
@@ -360,12 +363,6 @@
 
     loop(0, steps, work)
     gain_hop_one()
-    loop(held, steps - 1, give_back)
-    gain_hop_two()
-    third_after = min(THIRD_AFTER, owner_count)
-    give_back(steps - 1, 1, third_after)
-    gain_hop_three()
-    give_back(steps - 1, third_after, owner_count)
 
     remote(
         image_res.at[0, all_heads, other_rows],
@@ -394,6 +391,13 @@
     for copy in local_results:
         copy.start()
 
+    loop(held, steps - 1, give_back)
+    gain_hop_two()
+    third_after = min(THIRD_AFTER, owner_count)
+    give_back(steps - 1, 1, third_after)
+    gain_hop_three()
+    give_back(steps - 1, third_after, owner_count)
+
     pltpu.make_async_copy(third_others, third_others, gain_recv.at[2]).wait()
     gain = jnp.sum(gain_third[...], axis=0) / samples
     gain_out[0] = gain[:2]
@@ -431,10 +435,16 @@
 def put_out(count, *refs):
     results, outs, held = refs[:count], refs[count : 2 * count], refs[2 * count : 3 * count]
     semaphores = refs[-1]
-    reads = [
-        pltpu.make_async_copy(results[i], held[i], semaphores.at[0, i]) for i in range(count)
-    ]
-    writes = [pltpu.make_async_copy(held[i], outs[i], semaphores.at[1, i]) for i in range(count)]
+    reads, writes = [], []
+    for i in range(count):
+        long = max(range(results[i].ndim - 2), key=lambda d: results[i].shape[d])
+        pieces = PIECES if results[i].shape[long] % PIECES == 0 else 1
+        size = results[i].shape[long] // pieces
+        for j in range(pieces):
+            part = (slice(None),) * long + (pl.ds(j * size, size),)
+            src, mid, dst = results[i].at[part], held[i].at[part], outs[i].at[part]
+            reads.append(pltpu.make_async_copy(src, mid, semaphores.at[0, i, j]))
+            writes.append(pltpu.make_async_copy(mid, dst, semaphores.at[1, i, j]))
     for copy in reads:
         copy.start()
     for read, write in zip(reads, writes):
@@ -507,7 +517,7 @@
         out_shape=tuple(jax.ShapeDtypeStruct(r.shape, r.dtype) for r in results),
         in_specs=[anywhere] * len(results),
         out_specs=(anywhere,) * len(results),
-        scratch_shapes=[pltpu.VMEM(r.shape, r.dtype) for r in results] + [dma((2, len(results)))],
+        scratch_shapes=[pltpu.VMEM(r.shape, r.dtype) for r in results] + [dma((2, len(results), PIECES))],
         compiler_params=pltpu.CompilerParams(vmem_limit_bytes=VMEM_LIMIT),
     )(*results)
     return text_out, image_out, text_proj_grad, image_proj_grad, gain_grad

time: 90 us -> 90.5 us (level)
  no operation moved by 1% of the time
where the time goes in v4:
time: 90.5 us; the launch traced here: 90.4 us
  Pallas kernels  89.1 us (98%)
  between operations  1.29 us (1%)
    pallas_call x1, Pallas kernels, per_device(): pl.pallas_call(functools.partial(kernel, sizes), out_shape=(jax.ShapeDtyp...  86.5 us
    pallas_call x1, Pallas kernels, per_device(): pl.pallas_call(functools.partial(put_out, len(results)), out_shape=tuple(...  2.58 us

profile of v4, /device:TPU:1, one launch (start us, length us, event | category | flops | bytes accessed | tf_op | source)
XLA Modules:
  0.0 90.4 jit_solution(7135614122971084904)
XLA Ops:
  1.3 86.5 %shard_map.101 = (bf16[32,12,2,128]{3,2,1,0:T(2,128)(2,1)}, bf16[3,32,12,2,128]{4,3,2,1,0:T(2,128)(2,1)}, bf16[1,12,80,128]{3,2,1,0:T(8,128)(2,1)}, bf16[3,1,12,80,128]{4,3,2,1,0:T(8,128)(2,1)}, f32[2,2,128]{2,1,0:T(2,128)}) custom-call(bf16[3,32,12,2,128]{4,3,2,1,0:T(2,128)(2,1)} %text_proj.1, bf16[32,12,2,128]{3,2,1,0:T(2,128)(2,1)} %text_grad.1, ...), custom_call_target="tpu_custom_call" | custom-call | flops 764411904 | bytes 7077888 | tf_op jit(solution)/shard_map/pallas_call | solution.py:470
  87.8 2.6 %shard_map.102 = (bf16[32,12,2,128]{3,2,1,0:T(2,128)(2,1)}, bf16[3,32,12,2,128]{4,3,2,1,0:T(2,128)(2,1)}, bf16[1,12,80,128]{3,2,1,0:T(8,128)(2,1)}, bf16[3,1,12,80,128]{4,3,2,1,0:T(8,128)(2,1)}, f32[2,2,128]{2,1,0:T(2,128)}) custom-call(bf16[32,12,2,128]{3,2,1,0:T(2,128)(2,1)} %get-tuple-element.15.refs_0_, ...), custom_call_target="tpu_custom_call" | custom-call | tf_op jit(solution)/shard_map/pallas_call | solution.py:515
